TPU v7x, 256 devices: a whole 4x4x8 slice. The times are simulated.
256 devices in a mesh: dp: 16 (over z, core), tensor: 16 (over y, x).
Axes of the slice: x: 4, y: 4, z: 8, core: 2. Of those that a mesh axis runs over, the one named last changes fastest.
Arguments:
- activations: bfloat16 [36864, 8192], P('dp', 'tensor'), may hold values from -6 to 6
- out_grads: bfloat16 [36864, 28672], P('dp', 'tensor'), may hold values from -0.0546875 to 0.0546875
- basis: bfloat16 [8192, 256], P('tensor'), may hold values from -0.375 to 0.375
- first_moment: float32 [256, 28672], P('dp', 'tensor'), may hold values from -6 to 6
- second_moment: float32 [256, 28672], P('dp', 'tensor'), may hold values from 0.05 to 0.8
- reward_codes: int32 [36864], P('dp'), may hold values from 0 to 15
- token_ids: int32 [36864], P('dp'), may hold values from 0 to 128004, as said below
Outputs:
- new_first: float32 [256, 28672], P('dp', 'tensor')
- new_second: float32 [256, 28672], P('dp', 'tensor')
- weight_update: bfloat16 [8192, 28672], P('dp', 'tensor')
Inputs may be any that keep to these rules, and one draw needn't show every extreme that they name: `token_ids`: the id 128004 is the padding token; the first of each 2304 consecutive tokens is never padding.
All inputs are finite; a program needn't handle non-finite values.
Results may differ from a plain program's by a relative error of at most 0.019.
Values may be sent and summed in bfloat16 or wider, within the bound.
A program may use at most 64 MiB of HBM per device.

v0:
```python
import jax
import jax.numpy as jnp
from jax import lax
from jax.sharding import PartitionSpec as P

ADAM_STEP = 100
pad_token = 128004
reward_temp = 0.2
beta_one = 0.9
beta_two = 0.999
adam_eps = 1e-08


def filled_up(lines, size):
    spare = -len(lines) % size
    return jnp.pad(lines, [(0, spare)] + [(0, 0)] * (lines.ndim - 1))


def joined_along(parts, dim):
    parts = jnp.moveaxis(parts, 0, dim)
    lengths = parts.shape
    return parts.reshape(*lengths[:dim], lengths[dim] * lengths[dim + 1], *lengths[dim + 2 :])


def sent_to_all(shard, axis):
    size = lax.axis_size(axis)
    return lax.all_to_all(
        jnp.broadcast_to(shard[None], (size, *shard.shape)), axis, 0, 0, tiled=True
    )


def gather_directly(shard, axis, dim):
    return joined_along(sent_to_all(shard, axis), dim)


def split_up(shard, dim, size):
    before, after = (shard.shape[:dim], shard.shape[dim + 1 :])
    return jnp.moveaxis(shard.reshape(*before, size, -1, *after), dim, 0)


def sum_at_owner(shard, axis, dim):
    parts = split_up(shard, dim, lax.axis_size(axis))
    arrived = lax.all_to_all(parts, axis, split_axis=0, concat_axis=0, tiled=True)
    return arrived.astype(jnp.float32).sum(axis=0)


def total_of(shard, axes):
    lines = shard.reshape(-1, shard.shape[-1])
    padded = filled_up(lines, lax.axis_size(axes))
    whole = gather_directly(sum_at_owner(padded, axes, 0).astype(jnp.bfloat16), axes, 0)
    return lax.slice_in_dim(whole, 0, len(lines)).reshape(shard.shape).astype(jnp.float32)


def of_everyone(shard, axis):
    return sent_to_all(shard, axis).sum(axis=0)


def broadcast(shard, axis, root):
    return lax.dynamic_index_in_dim(lax.all_gather(shard, axis), root, 0, keepdims=False)


def local(activations, out_grads, basis, first_moment, second_moment, reward_codes, token_ids):
    data_count = lax.axis_size("dp")
    tensor_count = lax.axis_size("tensor")
    partial_value = jnp.dot(activations, basis, preferred_element_type=jnp.float32)
    projected = total_of(partial_value.astype(jnp.bfloat16), "tensor")
    unmasked = (token_ids != pad_token).astype(jnp.float32)
    weights = unmasked * jnp.exp(reward_temp * reward_codes.astype(jnp.float32))
    local_total = jnp.sum(weights)
    weighted = (weights[:, None] * projected).astype(jnp.bfloat16)
    raw_grad = lax.dot_general(
        weighted, out_grads, (((0,), (0,)), ((), ())), preferred_element_type=jnp.float32
    )
    normalizer = of_everyone(local_total, "dp")
    grad_rows = sum_at_owner(raw_grad.astype(jnp.bfloat16), "dp", 0)
    token_count = activations.shape[0] * data_count
    gradient = grad_rows * (token_count / normalizer)
    new_first = beta_one * first_moment + (1.0 - beta_one) * gradient
    new_second = beta_two * second_moment + (1.0 - beta_two) * gradient * gradient
    bias_one = 1.0 - beta_one**ADAM_STEP
    bias_two = 1.0 - beta_two**ADAM_STEP
    update = (new_first / bias_one / (jnp.sqrt(new_second / bias_two) + adam_eps)).astype(
        jnp.bfloat16
    )
    data_index = lax.axis_index("dp")
    owner_index = data_index * tensor_count // data_count
    owner_rows = broadcast(basis, "tensor", owner_index)
    summed = jnp.dot(
        owner_rows,
        lax.all_gather(update, "dp", axis=0, tiled=True),
        preferred_element_type=jnp.float32,
    )
    return (new_first, new_second, summed.astype(jnp.bfloat16))


def solution(mesh):
    return jax.shard_map(
        local,
        mesh=mesh,
        in_specs=(
            P("dp", "tensor"),
            P("dp", "tensor"),
            P("tensor", None),
            P("dp", "tensor"),
            P("dp", "tensor"),
            P("dp"),
            P("dp"),
        ),
        out_specs=(P("dp", "tensor"), P("dp", "tensor"), P("dp", "tensor")),
        check_vma=False,
    )
```

profile of v0, /device:TPU:1, one launch (start us, length us, event | category | flops | bytes accessed | tf_op | source)
XLA Modules:
  0.0 148.8 jit_solution(3367582259047807124)
XLA Ops:
  7.2 0.0 copy-start
  7.2 0.0 all-gather.3.cloned.1.call-start
  7.2 0.7 all-gather.3.cloned.1.call-update
  7.9 0.9 copy-done
  8.8 1.7 %convolution_convert_fusion = bf16[2304,256]{1,0:T(8,128)(2,1)S(1)} fusion(bf16[2304,512]{1,0:T(8,128)(2,1)S(1)} %copy-done, bf16[512,256]{1,0:T(8,128)(2,1)} %param.9), kind=kOutput, calls=%fused_computation | convolution fusion | flops 604569600 | bytes 3801088 | tf_op jit(solution)/shard_map/dot_general | solution.py:65
  10.6 26.5 %all_to_all.21 = bf16[16,144,256]{2,1,0:T(8,128)(2,1)S(1)} all-to-all(bf16[16,144,256]{2,1,0:T(8,128)(2,1)S(1)} %bitcast.14), channel_id=1, replica_groups=mesh['dp'=16,'tensor'=16] {'tensor'}, dimensions={0} | all-to-all | bytes 2359296 | tf_op jit(solution)/shard_map/all_to_all | solution.py:43
  37.1 0.8 reduce_sum.39
  37.9 2.0 %broadcast_in_dim.4 = bf16[16,144,256]{2,1,0:T(8,128)(2,1)} broadcast(bf16[144,256]{1,0:T(8,128)(2,1)} %reduce_sum.39), dimensions={1,2} | broadcast | bytes 1253376 | tf_op jit(solution)/shard_map/broadcast_in_dim | solution.py:28
  39.9 3.7 %all-to-all-start.1 = ((bf16[16,144,256]{2,1,0:T(8,128)(2,1)}), bf16[16,144,256]{2,1,0:T(8,128)(2,1)S(1)}, u32[]{:S(2)}, u32[]{:S(2)}) async-start(bf16[16,144,256]{2,1,0:T(8,128)(2,1)} %broadcast_in_dim.4), calls=%async_computation.1 | async-start | bytes 2359296 | tf_op jit(solution)/shard_map/all_to_all | solution.py:27
  43.6 1.3 fusion.8
  44.9 14.6 %all-to-all-done.1 = bf16[16,144,256]{2,1,0:T(8,128)(2,1)S(1)} async-done(((bf16[16,144,256]{2,1,0:T(8,128)(2,1)}), bf16[16,144,256]{2,1,0:T(8,128)(2,1)S(1)}, u32[]{:S(2)}, u32[]{:S(2)}) %all-to-all-start.1) | async-done | bytes 1179680 | tf_op jit(solution)/shard_map/all_to_all | solution.py:27
  59.6 1.2 broadcast_in_dim.5
  60.8 21.0 %all-to-all-start.3 = ((f32[16,1,1]{2,1,0:T(1,128)}), f32[16,1,1]{2,1,0:T(1,128)}, u32[]{:S(2)}, u32[]{:S(2)}) async-start(f32[16,1,1]{2,1,0:T(1,128)} %broadcast_in_dim.5), calls=%async_computation.3 | async-start | bytes 16384 | tf_op jit(solution)/shard_map/all_to_all | solution.py:27
  81.9 6.7 %convolution_convert_fusion.2 = bf16[256,1792]{1,0:T(8,128)(2,1)} fusion(bf16[2304,1792]{1,0:T(8,128)(2,1)} %param.8, bf16[2304,256]{1,0:T(8,128)(2,1)S(1)} %bitcast.12, f32[2304]{0:T(1024)S(1)} %get-tuple-element.7), kind=kOutput, calls=%fused_computation.2 | convolution fusion | flops 2116157440 | bytes 10363904 | tf_op jit(solution)/shard_map/dot_general | solution.py:71
  88.6 0.0 copy-start.1
  88.6 0.0 copy-start.2
  88.6 0.3 all-to-all-done.3
  88.9 7.0 %all-to-all-start.2 = ((bf16[16,16,1792]{2,1,0:T(8,128)(2,1)}), bf16[16,16,1792]{2,1,0:T(8,128)(2,1)S(1)}, u32[]{:S(2)}, u32[]{:S(2)}) async-start(bf16[16,16,1792]{2,1,0:T(8,128)(2,1)} %bitcast.13), calls=%async_computation.2 | async-start | bytes 1835008 | tf_op jit(solution)/shard_map/all_to_all | solution.py:43
  96.0 1.3 reduce_sum.42
  98.0 23.3 %all-to-all-done.2 = bf16[16,16,1792]{2,1,0:T(8,128)(2,1)S(1)} async-done(((bf16[16,16,1792]{2,1,0:T(8,128)(2,1)}), bf16[16,16,1792]{2,1,0:T(8,128)(2,1)S(1)}, u32[]{:S(2)}, u32[]{:S(2)}) %all-to-all-start.2) | async-done | bytes 917536 | tf_op jit(solution)/shard_map/all_to_all | solution.py:43
  121.2 0.1 convert_reduce_fusion
  121.4 0.0 copy-done.1
  121.4 0.0 copy-done.2
  121.4 0.8 divide_convert_fusion
  122.2 17.0 %all_gather.11 = bf16[256,1792]{1,0:T(8,128)(2,1)S(1)} all-gather(bf16[16,1792]{1,0:T(8,128)(2,1)S(1)} %get-tuple-element.3), channel_id=1, replica_groups=mesh['dp'=16,'tensor'=16] {'dp'}, dimensions={0}, use_global_device_ids=true | all-gather | bytes 974848 | tf_op jit(solution)/shard_map/all_gather | solution.py:90
  139.1 0.0 all-gather.3.cloned.1.call-done
  139.1 2.8 %convolution_convert_fusion.1 = bf16[512,1792]{1,0:T(8,128)(2,1)} fusion(bf16[256,1792]{1,0:T(8,128)(2,1)S(1)} %all_gather.11, bf16[16,512,256]{2,1,0:T(8,128)(2,1)} %bitcast.15, s32[]{:T(128)S(6)} %select_n.10), kind=kOutput, calls=%fused_computation.1 | convolution fusion | flops 470679552 | bytes 3014660 | tf_op jit(solution)/shard_map/dot_general | solution.py:88
Async XLA Ops:
  7.2 1.7 %copy-start = (bf16[2304,512]{1,0:T(8,128)(2,1)S(1)}, bf16[2304,512]{1,0:T(8,128)(2,1)}, u32[]{:S(2)}) copy-start(bf16[2304,512]{1,0:T(8,128)(2,1)} %param.7) | copy-start | bytes 7077892
  7.2 132.0 %all-gather.3.cloned.1.call-start = ((), (), s32[]{:S(2)}) async-start(), calls=%async_computation.4 | async-start | bytes 4456448 | tf_op jit(solution)/shard_map/all_gather | solution.py:59
  39.9 19.7 %all-to-all-start.1 = ((bf16[16,144,256]{2,1,0:T(8,128)(2,1)}), bf16[16,144,256]{2,1,0:T(8,128)(2,1)S(1)}, u32[]{:S(2)}, u32[]{:S(2)}) async-start(bf16[16,144,256]{2,1,0:T(8,128)(2,1)} %broadcast_in_dim.4), calls=%async_computation.1 | async-start | bytes 2359296 | tf_op jit(solution)/shard_map/all_to_all | solution.py:27
  60.8 28.1 %all-to-all-start.3 = ((f32[16,1,1]{2,1,0:T(1,128)}), f32[16,1,1]{2,1,0:T(1,128)}, u32[]{:S(2)}, u32[]{:S(2)}) async-start(f32[16,1,1]{2,1,0:T(1,128)} %broadcast_in_dim.5), calls=%async_computation.3 | async-start | bytes 16384 | tf_op jit(solution)/shard_map/all_to_all | solution.py:27
  88.6 32.8 %copy-start.1 = (f32[16,1792]{1,0:T(8,128)S(1)}, f32[16,1792]{1,0:T(8,128)}, u32[]{:S(2)}) copy-start(f32[16,1792]{1,0:T(8,128)} %param.11) | copy-start | bytes 344068
  88.6 32.8 %copy-start.2 = (f32[16,1792]{1,0:T(8,128)S(1)}, f32[16,1792]{1,0:T(8,128)}, u32[]{:S(2)}) copy-start(f32[16,1792]{1,0:T(8,128)} %param.10) | copy-start | bytes 344068
  88.9 32.3 %all-to-all-start.2 = ((bf16[16,16,1792]{2,1,0:T(8,128)(2,1)}), bf16[16,16,1792]{2,1,0:T(8,128)(2,1)S(1)}, u32[]{:S(2)}, u32[]{:S(2)}) async-start(bf16[16,16,1792]{2,1,0:T(8,128)(2,1)} %bitcast.13), calls=%async_computation.2 | async-start | bytes 1835008 | tf_op jit(solution)/shard_map/all_to_all | solution.py:43
Sparse Core Ops, SparseCore 0:
  10.4 67.8 all-gather.2
where the time goes:
time: 149 us
  blocking collectives  43.5 us (29%)
  waiting for transfers between devices  38.9 us (26%)
  starting transfers between devices  31.8 us (21%)
  between operations  14.8 us (10%)
  matrix products  11.3 us (8%)
  other arithmetic  4.34 us (3%)
  local copies, waits for them, and re-layouts  4.16 us (3%)
    all_to_all x1, blocking collectives, sum_at_owner(): lax.all_to_all(parts, axis, split_axis=0, concat_axis=0, tiled=True)  26.5 us
    all_to_all x2, starting transfers between devices, sent_to_all(): lax.all_to_all(jnp.broadcast_to(shard[None], (size, *shard.shape)), axis,...  24.7 us
    all_to_all x1, waiting for transfers between devices, sum_at_owner(): lax.all_to_all(parts, axis, split_axis=0, concat_axis=0, tiled=True)  23.3 us
    all_gather x1, blocking collectives, local(): lax.all_gather(update, 'dp', axis=0, tiled=True)  17 us
    all_to_all x2, waiting for transfers between devices, sent_to_all(): lax.all_to_all(jnp.broadcast_to(shard[None], (size, *shard.shape)), axis,...  15 us
    all_to_all x1, starting transfers between devices, sum_at_owner(): lax.all_to_all(parts, axis, split_axis=0, concat_axis=0, tiled=True)  7.04 us
    dot_general x1, matrix products, local(): lax.dot_general(weighted, out_grads, (((0,), (0,)), ((), ())), preferred_...  6.72 us
    broadcast_in_dim x2, local copies, waits for them, and re-layouts, sent_to_all(): jnp.broadcast_to(shard[None], (size, *shard.shape))  3.22 us
  transfers between devices with their start and end apart: 4, of which 3 were waited for; matrix products, arithmetic and copies ran while one was open for 11% of the time, Pallas kernels for 0%

commit v1 on v0

--- a/solution.py
+++ b/solution.py
@@ -87,7 +87,9 @@
     owner_rows = broadcast(basis, "tensor", owner_index)
     summed = jnp.dot(
         owner_rows,
-        lax.all_gather(update, "dp", axis=0, tiled=True),
+        jnp.concatenate(
+            lax.all_to_all(jnp.stack([update] * lax.axis_size("dp")), "dp", 0, 0), axis=0
+        ),
         preferred_element_type=jnp.float32,
     )
     return (new_first, new_second, summed.astype(jnp.bfloat16))

time: 149 us -> 162 us (1.087)
  waiting for transfers between devices: 38.9 us -> 63.9 us
  blocking collectives: 43.5 us -> 26.5 us
  starting transfers between devices: 31.8 us -> 35.5 us
    all_to_all x0 -> x1, waiting for transfers between devices: none -> 25.1 us  [local(): lax.all_to_all(jnp.stack([update] * lax.axis_size('dp')), 'dp', 0, 0)]
    all_gather x1 -> x0, blocking collectives: 17 us -> none  [local(): lax.all_gather(update, 'dp', axis=0, tiled=True)]
    all_to_all x0 -> x1, starting transfers between devices: none -> 3.53 us  [local(): lax.all_to_all(jnp.stack([update] * lax.axis_size('dp')), 'dp', 0, 0)]
  transfers between devices with their start and end apart: 4 -> 5, of which waited for: 3 -> 4; matrix products, arithmetic and copies ran while one was open for 11% -> 11% of each run, Pallas kernels for 0% -> 0%
where the time goes in v1:
time: 162 us; the launch traced here: 161 us
  waiting for transfers between devices  63.9 us (39%)
  starting transfers between devices  35.5 us (22%)
  blocking collectives  26.5 us (16%)
  between operations  14.8 us (9%)
  matrix products  11.3 us (7%)
  local copies, waits for them, and re-layouts  5.14 us (3%)
  other arithmetic  4.34 us (3%)
    all_to_all x1, blocking collectives, sum_at_owner(): lax.all_to_all(parts, axis, split_axis=0, concat_axis=0, tiled=True)  26.5 us
    all_to_all x1, waiting for transfers between devices, local(): lax.all_to_all(jnp.stack([update] * lax.axis_size('dp')), 'dp', 0, 0)  25.1 us
    all_to_all x2, starting transfers between devices, sent_to_all(): lax.all_to_all(jnp.broadcast_to(shard[None], (size, *shard.shape)), axis,...  24.7 us
    all_to_all x1, waiting for transfers between devices, sum_at_owner(): lax.all_to_all(parts, axis, split_axis=0, concat_axis=0, tiled=True)  23.3 us
    all_to_all x2, waiting for transfers between devices, sent_to_all(): lax.all_to_all(jnp.broadcast_to(shard[None], (size, *shard.shape)), axis,...  14.8 us
    all_to_all x1, starting transfers between devices, sum_at_owner(): lax.all_to_all(parts, axis, split_axis=0, concat_axis=0, tiled=True)  7.19 us
    dot_general x1, matrix products, local(): lax.dot_general(weighted, out_grads, (((0,), (0,)), ((), ())), preferred_...  6.72 us
    all_to_all x1, starting transfers between devices, local(): lax.all_to_all(jnp.stack([update] * lax.axis_size('dp')), 'dp', 0, 0)  3.53 us
  transfers between devices with their start and end apart: 5, of which 4 were waited for; matrix products, arithmetic and copies ran while one was open for 11% of the time, Pallas kernels for 0%

profile of v1, /device:TPU:1, one launch (start us, length us, event | category | flops | bytes accessed | tf_op | source)
XLA Modules:
  0.0 161.5 jit_solution(4987566184697905584)
XLA Ops:
  7.2 0.0 copy-start
  7.2 0.0 all-gather.3.cloned.1.call-start
  7.2 0.7 all-gather.3.cloned.1.call-update
  7.9 0.9 copy-done
  8.8 1.7 %convolution_convert_fusion = bf16[2304,256]{1,0:T(8,128)(2,1)S(1)} fusion(bf16[2304,512]{1,0:T(8,128)(2,1)S(1)} %copy-done, bf16[512,256]{1,0:T(8,128)(2,1)} %param.9), kind=kOutput, calls=%fused_computation | convolution fusion | flops 604569600 | bytes 3801088 | tf_op jit(solution)/shard_map/dot_general | solution.py:65
  10.6 26.5 %all_to_all.26 = bf16[16,144,256]{2,1,0:T(8,128)(2,1)S(1)} all-to-all(bf16[16,144,256]{2,1,0:T(8,128)(2,1)S(1)} %bitcast.16), channel_id=1, replica_groups=mesh['dp'=16,'tensor'=16] {'tensor'}, dimensions={0} | all-to-all | bytes 2359296 | tf_op jit(solution)/shard_map/all_to_all | solution.py:43
  37.1 0.8 reduce_sum.39
  37.9 2.0 %broadcast_in_dim.4 = bf16[16,144,256]{2,1,0:T(8,128)(2,1)} broadcast(bf16[144,256]{1,0:T(8,128)(2,1)} %reduce_sum.39), dimensions={1,2} | broadcast | bytes 1253376 | tf_op jit(solution)/shard_map/broadcast_in_dim | solution.py:28
  39.9 3.7 %all-to-all-start.1 = ((bf16[16,144,256]{2,1,0:T(8,128)(2,1)}), bf16[16,144,256]{2,1,0:T(8,128)(2,1)S(1)}, u32[]{:S(2)}, u32[]{:S(2)}) async-start(bf16[16,144,256]{2,1,0:T(8,128)(2,1)} %broadcast_in_dim.4), calls=%async_computation.1 | async-start | bytes 2359296 | tf_op jit(solution)/shard_map/all_to_all | solution.py:27
  43.6 1.3 fusion.8
  44.9 14.6 %all-to-all-done.1 = bf16[16,144,256]{2,1,0:T(8,128)(2,1)S(1)} async-done(((bf16[16,144,256]{2,1,0:T(8,128)(2,1)}), bf16[16,144,256]{2,1,0:T(8,128)(2,1)S(1)}, u32[]{:S(2)}, u32[]{:S(2)}) %all-to-all-start.1) | async-done | bytes 1179680 | tf_op jit(solution)/shard_map/all_to_all | solution.py:27
  59.6 1.2 broadcast_in_dim.5
  60.8 21.0 %all-to-all-start.3 = ((f32[16,1,1]{2,1,0:T(1,128)}), f32[16,1,1]{2,1,0:T(1,128)}, u32[]{:S(2)}, u32[]{:S(2)}) async-start(f32[16,1,1]{2,1,0:T(1,128)} %broadcast_in_dim.5), calls=%async_computation.3 | async-start | bytes 16384 | tf_op jit(solution)/shard_map/all_to_all | solution.py:27
  81.9 6.7 %convolution_convert_fusion.2 = bf16[256,1792]{1,0:T(8,128)(2,1)} fusion(bf16[2304,1792]{1,0:T(8,128)(2,1)} %param.8, bf16[2304,256]{1,0:T(8,128)(2,1)S(1)} %bitcast.13, f32[2304]{0:T(1024)S(1)} %get-tuple-element.7), kind=kOutput, calls=%fused_computation.2 | convolution fusion | flops 2116157440 | bytes 10363904 | tf_op jit(solution)/shard_map/dot_general | solution.py:71
  88.6 0.0 copy-start.1
  88.6 0.0 copy-start.2
  88.6 0.2 all-to-all-done.3
  88.8 7.2 %all-to-all-start.2 = ((bf16[16,16,1792]{2,1,0:T(8,128)(2,1)}), bf16[16,16,1792]{2,1,0:T(8,128)(2,1)S(1)}, u32[]{:S(2)}, u32[]{:S(2)}) async-start(bf16[16,16,1792]{2,1,0:T(8,128)(2,1)} %bitcast.15), calls=%async_computation.2 | async-start | bytes 1835008 | tf_op jit(solution)/shard_map/all_to_all | solution.py:43
  96.0 1.3 reduce_sum.42
  98.0 23.3 %all-to-all-done.2 = bf16[16,16,1792]{2,1,0:T(8,128)(2,1)S(1)} async-done(((bf16[16,16,1792]{2,1,0:T(8,128)(2,1)}), bf16[16,16,1792]{2,1,0:T(8,128)(2,1)S(1)}, u32[]{:S(2)}, u32[]{:S(2)}) %all-to-all-start.2) | async-done | bytes 917536 | tf_op jit(solution)/shard_map/all_to_all | solution.py:43
  121.2 0.1 convert_reduce_fusion
  121.4 0.0 copy-done.1
  121.4 0.0 copy-done.2
  121.4 0.8 divide_convert_fusion
  122.2 1.0 stack.2
  123.1 3.5 %all-to-all-start.4 = ((bf16[16,16,1792]{2,1,0:T(8,128)(2,1)}), bf16[16,16,1792]{2,1,0:T(8,128)(2,1)S(1)}, u32[]{:S(2)}, u32[]{:S(2)}) async-start(bf16[16,16,1792]{2,1,0:T(8,128)(2,1)} %stack.2), calls=%async_computation.4 | async-start | bytes 1835008 | tf_op jit(solution)/shard_map/all_to_all | solution.py:91
  126.7 25.1 %all-to-all-done.4 = bf16[16,16,1792]{2,1,0:T(8,128)(2,1)S(1)} async-done(((bf16[16,16,1792]{2,1,0:T(8,128)(2,1)}), bf16[16,16,1792]{2,1,0:T(8,128)(2,1)S(1)}, u32[]{:S(2)}, u32[]{:S(2)}) %all-to-all-start.4) | async-done | bytes 917536 | tf_op jit(solution)/shard_map/all_to_all | solution.py:91
  151.8 0.0 all-gather.3.cloned.1.call-done
  151.8 2.8 %convolution_convert_fusion.1 = bf16[512,1792]{1,0:T(8,128)(2,1)} fusion(bf16[256,1792]{1,0:T(8,128)(2,1)S(1)} %bitcast.14, bf16[16,512,256]{2,1,0:T(8,128)(2,1)} %bitcast.17, s32[]{:T(128)S(6)} %select_n.10), kind=kOutput, calls=%fused_computation.1 | convolution fusion | flops 470679552 | bytes 3014660 | tf_op jit(solution)/shard_map/dot_general | solution.py:88
Async XLA Ops:
  7.2 1.7 %copy-start = (bf16[2304,512]{1,0:T(8,128)(2,1)S(1)}, bf16[2304,512]{1,0:T(8,128)(2,1)}, u32[]{:S(2)}) copy-start(bf16[2304,512]{1,0:T(8,128)(2,1)} %param.7) | copy-start | bytes 7077892
  7.2 144.6 %all-gather.3.cloned.1.call-start = ((), (), s32[]{:S(2)}) async-start(), calls=%async_computation.5 | async-start | bytes 4456448 | tf_op jit(solution)/shard_map/all_gather | solution.py:59
  39.9 19.7 %all-to-all-start.1 = ((bf16[16,144,256]{2,1,0:T(8,128)(2,1)}), bf16[16,144,256]{2,1,0:T(8,128)(2,1)S(1)}, u32[]{:S(2)}, u32[]{:S(2)}) async-start(bf16[16,144,256]{2,1,0:T(8,128)(2,1)} %broadcast_in_dim.4), calls=%async_computation.1 | async-start | bytes 2359296 | tf_op jit(solution)/shard_map/all_to_all | solution.py:27
  60.8 27.9 %all-to-all-start.3 = ((f32[16,1,1]{2,1,0:T(1,128)}), f32[16,1,1]{2,1,0:T(1,128)}, u32[]{:S(2)}, u32[]{:S(2)}) async-start(f32[16,1,1]{2,1,0:T(1,128)} %broadcast_in_dim.5), calls=%async_computation.3 | async-start | bytes 16384 | tf_op jit(solution)/shard_map/all_to_all | solution.py:27
  88.6 32.8 %copy-start.1 = (f32[16,1792]{1,0:T(8,128)S(1)}, f32[16,1792]{1,0:T(8,128)}, u32[]{:S(2)}) copy-start(f32[16,1792]{1,0:T(8,128)} %param.11) | copy-start | bytes 344068
  88.6 32.8 %copy-start.2 = (f32[16,1792]{1,0:T(8,128)S(1)}, f32[16,1792]{1,0:T(8,128)}, u32[]{:S(2)}) copy-start(f32[16,1792]{1,0:T(8,128)} %param.10) | copy-start | bytes 344068
  88.8 32.5 %all-to-all-start.2 = ((bf16[16,16,1792]{2,1,0:T(8,128)(2,1)}), bf16[16,16,1792]{2,1,0:T(8,128)(2,1)S(1)}, u32[]{:S(2)}, u32[]{:S(2)}) async-start(bf16[16,16,1792]{2,1,0:T(8,128)(2,1)} %bitcast.15), calls=%async_computation.2 | async-start | bytes 1835008 | tf_op jit(solution)/shard_map/all_to_all | solution.py:43
  123.1 28.6 %all-to-all-start.4 = ((bf16[16,16,1792]{2,1,0:T(8,128)(2,1)}), bf16[16,16,1792]{2,1,0:T(8,128)(2,1)S(1)}, u32[]{:S(2)}, u32[]{:S(2)}) async-start(bf16[16,16,1792]{2,1,0:T(8,128)(2,1)} %stack.2), calls=%async_computation.4 | async-start | bytes 1835008 | tf_op jit(solution)/shard_map/all_to_all | solution.py:91
Sparse Core Ops, SparseCore 0:
  10.4 67.8 all-gather.2
